TPU v7x, 32 devices: a whole 2x2x4 slice. The times are simulated.
32 devices in a mesh: row: 8 (over y, x, core), col: 4 (over z).
Axes of the slice: x: 2, y: 2, z: 4, core: 2. Of those that a mesh axis runs over, the one named last changes fastest.
Arguments:
- hidden: bfloat16 [2048, 14336], P('col', 'row'), may hold values from -6 to 6
- grad_out: bfloat16 [2048, 8192], P('row', 'col'), may hold values from -6 to 6
- weight_blocks: bfloat16 [8, 1792, 4096], P('row', 'col'), may hold values from -0.09375 to 0.09375
- block_index: int32 [8, 1792], P('row', 'col'), may hold values from 0 to 895, as said below
- block_count: int32 [8, 4], P('row', 'col'), may hold values from 1 to 448, as said below
Outputs:
- output: bfloat16 [2048, 8192], P('row', 'col')
- input_grad: bfloat16 [2048, 14336], P('col', 'row')
- weight_grad: bfloat16 [8, 1792, 4096], P('row', 'col')
Inputs may be any that keep to these rules, and one draw needn't show every extreme that they name: `block_index`: within one tile the 448 entries are different block positions; slots at or past the tile's block_count are unused. `block_count`: live slots fill each tile from slot 0; some tile is full in every draw.
All inputs are finite; a program needn't handle non-finite values.
Results may differ from a plain program's by a relative error of at most 0.012.
Values may be sent and summed in bfloat16 or wider, within the bound.
A program may use at most 192 MiB of HBM per device.

v0:
```python
import math

import jax
import jax.numpy as jnp
from jax import lax
from jax.sharding import PartitionSpec as P

BLOCK = 64


def dense_tile(slots, index, live, row_blocks, col_blocks):
    positions = jnp.arange(row_blocks * col_blocks, dtype=jnp.int32)
    onehot = ((positions[:, None] == index[None, :]) & live[None, :]).astype(jnp.bfloat16)
    flat = jnp.dot(onehot, slots, preferred_element_type=jnp.float32).astype(jnp.bfloat16)
    return (
        flat.reshape(row_blocks, col_blocks, BLOCK, BLOCK)
        .transpose(0, 2, 1, 3)
        .reshape(row_blocks * BLOCK, col_blocks * BLOCK)
    )


def body(hidden, grad_out, weight_blocks, block_index, block_count):
    row_blocks = hidden.shape[1] // BLOCK
    col_blocks = grad_out.shape[1] // BLOCK
    slots = weight_blocks[0]
    index = block_index[0]
    filled = block_count[0, 0]
    capacity = slots.shape[0]
    live = jnp.arange(capacity, dtype=jnp.int32) < filled
    h_all = lax.all_gather(hidden, "col", axis=0, tiled=True)
    g_all = lax.all_gather(grad_out, "row", axis=0, tiled=True)
    tokens = h_all.shape[0]
    factor = 1.0 / math.sqrt(tokens)
    tile = dense_tile(slots, index, live, row_blocks, col_blocks)
    wide = (
        lax.dot_general(h_all, g_all, (((0,), (0,)), ((), ())), preferred_element_type=jnp.float32)
        * factor
    )
    blocks = (
        wide.reshape(row_blocks, BLOCK, col_blocks, BLOCK)
        .transpose(0, 2, 1, 3)
        .reshape(row_blocks * col_blocks, BLOCK * BLOCK)
    )
    picked = jnp.take(blocks, index, axis=0) * live[:, None].astype(jnp.float32)
    slot_grads = picked.astype(jnp.bfloat16)
    rows = h_all
    output = lax.psum_scatter(
        jnp.dot(rows, tile, preferred_element_type=jnp.float32).astype(jnp.bfloat16),
        "row",
        scatter_dimension=0,
        tiled=True,
    )
    rows = g_all
    input_grad = lax.psum_scatter(
        lax.dot_general(
            rows, tile, (((1,), (1,)), ((), ())), preferred_element_type=jnp.float32
        ).astype(jnp.bfloat16),
        "col",
        scatter_dimension=0,
        tiled=True,
    )
    return (output, input_grad, slot_grads[None])


def solution(mesh):
    return jax.shard_map(
        body,
        mesh=mesh,
        in_specs=(
            P("col", "row"),
            P("row", "col"),
            P("row", "col", None),
            P("row", "col"),
            P("row", "col"),
        ),
        out_specs=(P("row", "col"), P("col", "row"), P("row", "col", None)),
        check_vma=False,
    )
```

profile of v0, /device:TPU:0, one launch (start us, length us, event | category | flops | bytes accessed | tf_op | source)
XLA Modules:
  0.0 414.5 jit_solution(14650109789261039076)
XLA Ops:
  7.2 0.0 all-gather.3.cloned.1.call-start
  7.2 0.7 all-gather.3.cloned.1.call-update
  7.9 0.0 all-gather.5.cloned.1.call-start
  7.9 0.7 all-gather.5.cloned.1.call-update
  8.6 0.0 reduce-scatter.3.cloned.1.call-start
  9.4 8.0 %convolution_convert_fusion.1 = bf16[896,4096]{1,0:T(8,128)(2,1)} fusion(bf16[1,448,4096]{2,1,0:T(8,128)(2,1)} %param.7, s32[448]{0:T(512)} %bitcast.37, pred[448]{0:T(512)(128)(4,1)S(1)} %iota_compare_fusion.1), kind=kOutput, calls=%fused_computation.8 | convolution fusion | flops 3292807168 | bytes 11012288 | tf_op jit(solution)/shard_map/dot_general | solution.py:14
  17.4 21.0 %reshape.110 = bf16[28,32,64,64]{3,2,1,0:T(8,128)(2,1)} reshape(bf16[896,4096]{1,0:T(8,128)(2,1)} %convolution_convert_fusion.1) | data formatting | bytes 14680064 | tf_op jit(solution)/shard_map/reshape | solution.py:16
  38.3 16.6 %copy.16 = bf16[28,32,64,64]{3,1,2,0:T(8,128)(2,1)} copy(bf16[28,32,64,64]{3,2,1,0:T(8,128)(2,1)} %reshape.110) | data formatting | bytes 14680064 | tf_op jit(solution)/shard_map/reshape | solution.py:16
  54.9 20.8 %reshape.111 = bf16[1792,2048]{1,0:T(8,128)(2,1)} reshape(bf16[28,64,32,64]{3,2,1,0:T(8,128)(2,1)} %bitcast.35) | data formatting | bytes 14680064 | tf_op jit(solution)/shard_map/reshape | solution.py:18
  75.8 69.0 %all-gather.3.cloned.1.call-done = bf16[2048,1792]{1,0:T(8,128)(2,1)} async-done(((bf16[512,1792]{1,0:T(8,128)(2,1)}), bf16[2048,1792]{1,0:T(8,128)(2,1)}) %all-gather.3.cloned.1.call-update) | async-done | bytes 7340048 | tf_op jit(solution)/shard_map/all_gather | solution.py:30
  144.8 21.3 %convert_bitcast_fusion = bf16[2048,2048]{0,1:T(8,128)(2,1)} fusion(bf16[1792,2048]{1,0:T(8,128)(2,1)} %reshape.111, bf16[2048,1792]{1,0:T(8,128)(2,1)} %all-gather.3.cloned.1.call-done), kind=kOutput, calls=%fused_computation.3 | convolution fusion | flops 15036579840 | bytes 23068672 | tf_op jit(solution)/shard_map/dot_general | solution.py:48
  166.1 0.0 reduce-scatter.3.cloned.1.call-update
  166.1 0.2 reduce-scatter.5.cloned.1.call-start
  166.3 33.0 %all-gather.5.cloned.1.call-done = bf16[2048,2048]{1,0:T(8,128)(2,1)} async-done(((bf16[256,2048]{1,0:T(8,128)(2,1)}), bf16[2048,2048]{1,0:T(8,128)(2,1)}) %all-gather.5.cloned.1.call-update) | async-done | bytes 8388624 | tf_op jit(solution)/shard_map/all_gather | solution.py:31
  199.3 21.4 %fusion.2 = bf16[2048,1792]{0,1:T(8,128)(2,1)} fusion(bf16[1792,2048]{1,0:T(8,128)(2,1)} %reshape.111, bf16[2048,2048]{1,0:T(8,128)(2,1)} %all-gather.5.cloned.1.call-done), kind=kOutput, calls=%fused_computation.9 | convolution fusion | flops 15036055552 | bytes 23068672 | tf_op jit(solution)/shard_map/dot_general | solution.py:55
  220.7 0.0 copy-start
  220.7 0.0 reduce-scatter.5.cloned.1.call-update
  220.8 0.7 copy-done
  221.4 21.7 %convolution_multiply_fusion = f32[1792,2048]{1,0:T(8,128)} fusion(bf16[2048,1792]{1,0:T(8,128)(2,1)} %all-gather.3.cloned.1.call-done, bf16[2048,2048]{1,0:T(8,128)(2,1)} %all-gather.5.cloned.1.call-done), kind=kOutput, calls=%fused_computation.2 | convolution fusion | flops 15036055552 | bytes 30408704 | tf_op jit(solution)/shard_map/dot_general | solution.py:36
  243.2 24.4 %reshape.112 = f32[28,64,32,64]{3,2,1,0:T(8,128)} reshape(f32[1792,2048]{1,0:T(8,128)} %convolution_multiply_fusion) | data formatting | bytes 29360128 | tf_op jit(solution)/shard_map/reshape | solution.py:40
  267.6 29.1 %copy.12 = f32[28,32,64,64]{3,2,1,0:T(8,128)} copy(f32[28,32,64,64]{3,1,2,0:T(8,128)} %bitcast.34) | data formatting | bytes 29360128 | tf_op jit(solution)/shard_map/transpose | solution.py:41
  296.7 24.8 %reshape.113 = f32[896,4096]{1,0:T(8,128)} reshape(f32[28,32,64,64]{3,2,1,0:T(8,128)} %copy.12) | data formatting | bytes 29360128 | tf_op jit(solution)/shard_map/reshape | solution.py:42
  321.5 13.7 %gather_fusion = f32[448,4096]{1,0:T(8,128)} fusion(f32[896,4096]{1,0:T(8,128)} %reshape.113, s32[1024]{0:T(1024)S(1)} %pad_clamp_fusion), kind=kCustom, calls=%fused_computation | custom fusion | bytes 14681856 | tf_op jit(solution)/shard_map/jit(_take)/gather | solution.py:44
  335.2 6.6 %fusion.1 = bf16[1,448,4096]{2,1,0:T(8,128)(2,1)} fusion(f32[448,4096]{1,0:T(8,128)} %gather_fusion, f32[448]{0:T(512)S(1)} %get-tuple-element.10, pred[448]{0:T(512)(128)(4,1)S(1)} %get-tuple-element.9), kind=kLoop, calls=%fused_computation.7 | loop fusion | flops 5505024 | bytes 11012288 | tf_op jit(solution)/shard_map/convert_element_type | solution.py:45
  341.8 0.0 reduce-scatter.3.cloned.1.call-done
  341.8 2.3 copy.13
  344.1 60.1 %reduce-scatter.5.cloned.1.call-done = bf16[512,1792]{0,1:T(8,128)(2,1)} async-done(((bf16[2048,1792]{0,1:T(8,128)(2,1)}), bf16[512,1792]{0,1:T(8,128)(2,1)}) %reduce-scatter.5.cloned.1.call-update) | async-done | bytes 1835024 | tf_op jit(solution)/shard_map/reduce_scatter | solution.py:54
  404.1 3.8 copy.14
  (4 shorter events, 0.0 us)
Async XLA Ops:
  7.2 137.6 %all-gather.3.cloned.1.call-start = ((), (), s32[]{:S(2)}) async-start(), calls=%async_computation.2 | async-start | bytes 9175040 | tf_op jit(solution)/shard_map/all_gather | solution.py:30
  7.9 191.4 %all-gather.5.cloned.1.call-start = ((), (), s32[]{:S(2)}) async-start(), calls=%async_computation.4 | async-start | bytes 9437184 | tf_op jit(solution)/shard_map/all_gather | solution.py:31
  8.6 333.1 %reduce-scatter.3.cloned.1.call-start = ((), (), s32[]{:S(2)}) async-start(), calls=%async_computation.3 | async-start | bytes 9437184 | tf_op jit(solution)/shard_map/reduce_scatter | solution.py:47
  166.1 238.0 %reduce-scatter.5.cloned.1.call-start = ((), (), s32[]{:S(2)}) async-start(), calls=%async_computation.5 | async-start | bytes 9175040 | tf_op jit(solution)/shard_map/reduce_scatter | solution.py:54
  220.7 0.7 copy-start
Sparse Core Ops, SparseCore 0:
  9.6 135.1 all-gather.2
  146.7 52.6 all-gather.4
  202.8 71.2 reduce-scatter.2
  276.4 127.7 reduce-scatter.4
where the time goes:
time: 417 us; the launch traced here: 414 us
  waiting for transfers between devices  164 us (39%)
  local copies, waits for them, and re-layouts  157 us (38%)
  matrix products  72.4 us (17%)
  between operations  14.4 us (3%)
  other arithmetic  6.6 us (2%)
    all_gather x1, waiting for transfers between devices, body(): h_all = lax.all_gather(hidden, 'col', axis=0, tiled=True)  69 us
    reduce_scatter x1, waiting for transfers between devices, body(): lax.psum_scatter(lax.dot_general(rows, tile, (((1,), (1,)), ((), ())), pr...  60.1 us
    reshape x2, local copies, waits for them, and re-layouts, dense_tile(): flat.reshape(row_blocks, col_blocks, BLOCK, BLOCK).transpose(0, 2, 1, 3)  37.6 us
    all_gather x1, waiting for transfers between devices, body(): g_all = lax.all_gather(grad_out, 'row', axis=0, tiled=True)  33 us
    transpose x1, local copies, waits for them, and re-layouts, body(): blocks = wide.reshape(row_blocks, BLOCK, col_blocks, BLOCK).transpose(0,...  29.1 us
    reshape x1, local copies, waits for them, and re-layouts, body(): blocks = wide.reshape(row_blocks, BLOCK, col_blocks, BLOCK).transpose(0,...  24.8 us
    reshape x1, local copies, waits for them, and re-layouts, body(): wide.reshape(row_blocks, BLOCK, col_blocks, BLOCK).transpose(0, 2, 1, 3)  24.4 us
    dot_general x1, matrix products, body(): lax.dot_general(h_all, g_all, (((0,), (0,)), ((), ())), preferred_element...  21.7 us
  transfers between devices with their start and end apart: 4, of which 3 were waited for; matrix products, arithmetic and copies ran while one was open for 56% of the time, Pallas kernels for 0%

commit v1 on v0

v1 whole, which is shorter than its diff:
```python
import math

import jax
import jax.numpy as jnp
from jax import lax
from jax.experimental import pallas as pl
from jax.experimental.pallas import tpu as pltpu
from jax.sharding import PartitionSpec as P

BLOCK = 64
UNROLL = 4
CORE, X, Y = 1, 2, 4


def dense_tile(slots, index, live, row_blocks, col_blocks):
    positions = jnp.arange(row_blocks * col_blocks, dtype=jnp.int32)
    onehot = ((positions[:, None] == index[None, :]) & live[None, :]).astype(jnp.bfloat16)
    flat = jnp.dot(onehot, slots, preferred_element_type=jnp.float32).astype(jnp.bfloat16)
    return (
        flat.reshape(row_blocks, col_blocks, BLOCK, BLOCK)
        .transpose(0, 2, 1, 3)
        .reshape(row_blocks * BLOCK, col_blocks * BLOCK)
    )


def pick_kernel(col_blocks, capacity, index_ref, count_ref, wide_ref, out_ref, pair_ref):
    half = BLOCK // 2
    lane = lax.broadcasted_iota(jnp.int32, (half, 2 * BLOCK), 1)
    count = count_ref[0]

    def step(i, carry):
        for u in range(UNROLL):
            s = i * UNROLL + u
            k = index_ref[s]
            top = pl.multiple_of((k // col_blocks) * BLOCK, BLOCK)
            col = k % col_blocks
            left = pl.multiple_of((col // 2) * (2 * BLOCK), 2 * BLOCK)
            pair_ref[u] = wide_ref[pl.ds(top, BLOCK), pl.ds(left, 2 * BLOCK)]
            even = pair_ref[u, pl.ds(0, half, stride=2), :]
            odd = pair_ref[u, pl.ds(1, half, stride=2), :]
            first = jnp.where(lane < BLOCK, even, pltpu.roll(odd, BLOCK, 1))
            second = jnp.where(lane < BLOCK, pltpu.roll(even, BLOCK, 1), odd)
            block = jnp.where(col % 2 == 0, first, second)
            out_ref[s] = jnp.where(s < count, block, 0.0).astype(jnp.bfloat16)
        return carry

    lax.fori_loop(0, capacity // UNROLL, step, 0)


def pick_blocks(wide, index, count, col_blocks):
    capacity = index.shape[0]
    out = pl.pallas_call(
        lambda *refs: pick_kernel(col_blocks, capacity, *refs),
        out_shape=jax.ShapeDtypeStruct((capacity, BLOCK // 2, 2 * BLOCK), jnp.bfloat16),
        in_specs=[
            pl.BlockSpec(memory_space=pltpu.SMEM),
            pl.BlockSpec(memory_space=pltpu.SMEM),
            pl.BlockSpec(memory_space=pltpu.VMEM),
        ],
        out_specs=pl.BlockSpec(memory_space=pltpu.VMEM),
        scratch_shapes=[pltpu.VMEM((UNROLL, BLOCK, 2 * BLOCK), jnp.float32)],
        compiler_params=pltpu.CompilerParams(vmem_limit_bytes=40 * 1024 * 1024),
        cost_estimate=pl.CostEstimate(
            flops=0, bytes_accessed=3 * wide.size * 4, transcendentals=0
        ),
    )(index, count, wide)
    return out.reshape(capacity, BLOCK * BLOCK)


def swap(x, mask):
    return lax.ppermute(x, "row", [(r, r ^ mask) for r in range(8)])


def gather_row(g):
    me = lax.axis_index("row")
    half = g.shape[0] // 2
    gx, gy = swap(g, X), swap(g, Y)
    first = swap(gx[:half], Y)
    last = swap(gy[half:], X)
    mine = {0: g, X: gx, Y: gy}
    parts = [(m, 0, p) for m, p in mine.items()]
    parts += [(m ^ CORE, 0, swap(p, CORE)) for m, p in mine.items()]
    parts += [(X ^ Y, 0, first), (X ^ Y, half, last)]
    parts += [(X ^ Y ^ CORE, 0, swap(first, CORE)), (X ^ Y ^ CORE, half, swap(last, CORE))]
    whole = jnp.zeros((8 * g.shape[0], g.shape[1]), g.dtype)
    for m, start, p in parts:
        whole = lax.dynamic_update_slice(whole, p, ((me ^ m) * g.shape[0] + start, 0))
    return whole


def pick(x, i, axis):
    return lax.dynamic_index_in_dim(x, i, axis, keepdims=False)


def project_scatter_row(h_all, tile):
    me = lax.axis_index("row")
    core, x, y = me & 1, (me >> 1) & 1, (me >> 2) & 1
    share = h_all.shape[0] // 8
    split = h_all.reshape(4, 2, share, h_all.shape[1])
    width = tile.shape[1]
    mid = width // 2

    def product(which):
        rows = pick(split, which, 1).reshape(4 * share, -1)
        return jnp.dot(rows, tile, preferred_element_type=jnp.float32).astype(jnp.bfloat16)

    got = swap(product(1 - core), CORE)
    total = product(core).astype(jnp.float32) + got.astype(jnp.float32)
    total = total.astype(jnp.bfloat16).reshape(2, 2, share, width)
    a, b = total[..., :mid], total[..., mid:]

    def fold(v, axis, bit, mask):
        got = swap(pick(v, 1 - bit, axis), mask)
        return (pick(v, bit, axis).astype(jnp.float32) + got.astype(jnp.float32)).astype(
            jnp.bfloat16
        )

    a = fold(a, 1, x, X)
    b = fold(b, 0, y, Y)
    a = fold(a, 0, y, Y)
    b = fold(b, 0, x, X)
    return jnp.concatenate([a, b], axis=-1)


def body(small, hidden, grad_out, weight_blocks, block_index, block_count):
    row_blocks = hidden.shape[1] // BLOCK
    col_blocks = grad_out.shape[1] // BLOCK
    slots = weight_blocks[0]
    index = block_index[0]
    filled = block_count[0, 0]
    capacity = slots.shape[0]
    live = jnp.arange(capacity, dtype=jnp.int32) < filled
    h_all = lax.all_gather(hidden, "col", axis=0, tiled=True)
    if small:
        g_all = gather_row(grad_out)
    else:
        g_all = lax.all_gather(grad_out, "row", axis=0, tiled=True)
    tokens = h_all.shape[0]
    factor = 1.0 / math.sqrt(tokens)
    tile = dense_tile(slots, index, live, row_blocks, col_blocks)
    input_grad = lax.psum_scatter(
        lax.dot_general(
            g_all, tile, (((1,), (1,)), ((), ())), preferred_element_type=jnp.float32
        ).astype(jnp.bfloat16),
        "col",
        scatter_dimension=0,
        tiled=True,
    )
    if small:
        output = project_scatter_row(h_all, tile)
    else:
        output = lax.psum_scatter(
            jnp.dot(h_all, tile, preferred_element_type=jnp.float32).astype(jnp.bfloat16),
            "row",
            scatter_dimension=0,
            tiled=True,
        )
    wide = (
        lax.dot_general(h_all, g_all, (((0,), (0,)), ((), ())), preferred_element_type=jnp.float32)
        * factor
    )
    slot_grads = pick_blocks(wide, index, block_count[0], col_blocks)
    return (output, input_grad, slot_grads[None])


def solution(mesh):
    small = mesh.shape["row"] == 8

    def local(*args):
        return body(small, *args)

    return jax.shard_map(
        local,
        mesh=mesh,
        in_specs=(
            P("col", "row"),
            P("row", "col"),
            P("row", "col", None),
            P("row", "col"),
            P("row", "col"),
        ),
        out_specs=(P("row", "col"), P("col", "row"), P("row", "col", None)),
        check_vma=False,
    )
```

time: 417 us -> 287 us (0.69)
  waiting for transfers between devices: 164 us -> 64.1 us
  local copies, waits for them, and re-layouts: 157 us -> 96.8 us
  Pallas kernels: 0 us -> 19.8 us
  starting transfers between devices: 0.34 us -> 13.1 us
    all_gather x1, waiting for transfers between devices: 69 us -> 0.02 us  [body(): h_all = lax.all_gather(hidden, 'col', axis=0, tiled=True)]
    ppermute x0 -> x14, waiting for transfers between devices: none -> 58.4 us  [swap(): return lax.ppermute(x, 'row', [(r, r ^ mask) for r in range(8)])]
    reduce_scatter x2 -> x1, waiting for transfers between devices: 60.1 us -> 5.01 us  [body(): lax.psum_scatter(lax.dot_general(g_all, tile, (((1,), (1,)), ((), ())), p...]
    reshape x2 -> x0, local copies, waits for them, and re-layouts: 49.2 us -> none  [the longest x1 24.8 us: body(): blocks = wide.reshape(row_blocks, BLOCK, col_blocks, BLOCK).transpose(0,...]
    all_gather x1 -> x0, waiting for transfers between devices: 33 us -> none  [body(): g_all = lax.all_gather(grad_out, 'row', axis=0, tiled=True)]
    transpose x1 -> x0, local copies, waits for them, and re-layouts: 29.1 us -> none  [body(): blocks = wide.reshape(row_blocks, BLOCK, col_blocks, BLOCK).transpose(0,...]
    pallas_call x0 -> x1, Pallas kernels: none -> 19.8 us  [pick_blocks(): pl.pallas_call(lambda *refs: pick_kernel(col_blocks, capacity, *refs), ou...]
    gather x1 -> x0, local copies, waits for them, and re-layouts: 13.7 us -> none  [body(): picked = jnp.take(blocks, index, axis=0) * live[:, None].astype(jnp.float32)]
  transfers between devices with their start and end apart: 4 -> 16, of which waited for: 3 -> 6; matrix products, arithmetic and copies ran while one was open for 56% -> 59% of each run, Pallas kernels for 0% -> 7%
where the time goes in v1:
time: 287 us; the launch traced here: 285 us
  local copies, waits for them, and re-layouts  96.8 us (34%)
  matrix products  70.1 us (24%)
  waiting for transfers between devices  64.1 us (22%)
  Pallas kernels  19.8 us (7%)
  between operations  14.9 us (5%)
  starting transfers between devices  13.1 us (5%)
  other arithmetic  6.1 us (2%)
    ppermute x14, waiting for transfers between devices, swap(): return lax.ppermute(x, 'row', [(r, r ^ mask) for r in range(8)])  58.4 us
    reshape x2, local copies, waits for them, and re-layouts, dense_tile(): flat.reshape(row_blocks, col_blocks, BLOCK, BLOCK).transpose(0, 2, 1, 3)  37.6 us
    dot_general x1, matrix products, body(): lax.dot_general(h_all, g_all, (((0,), (0,)), ((), ())), preferred_element...  21.7 us
    dot_general x2, matrix products, product(): jnp.dot(rows, tile, preferred_element_type=jnp.float32).astype(jnp.bfloat16)  21.1 us
    reshape x1, local copies, waits for them, and re-layouts, dense_tile(): return flat.reshape(row_blocks, col_blocks, BLOCK, BLOCK).transpose(0, 2,...  20.8 us
    pallas_call x1, Pallas kernels, pick_blocks(): pl.pallas_call(lambda *refs: pick_kernel(col_blocks, capacity, *refs), ou...  19.8 us
    dot_general x1, matrix products, body(): lax.dot_general(g_all, tile, (((1,), (1,)), ((), ())), preferred_element_...  19.3 us
    dynamic_update_slice x10, local copies, waits for them, and re-layouts, gather_row(): lax.dynamic_update_slice(whole, p, ((me ^ m) * g.shape[0] + start, 0))  13.5 us
  transfers between devices with their start and end apart: 16, of which 6 were waited for; matrix products, arithmetic and copies ran while one was open for 59% of the time, Pallas kernels for 7%

profile of v1, /device:TPU:0, one launch (start us, length us, event | category | flops | bytes accessed | tf_op | source)
XLA Modules:
  0.0 284.9 jit_solution(9483107233374009367)
XLA Ops:
  7.9 3.0 %collective-permute-start.5 = (bf16[256,2048]{1,0:T(8,128)(2,1)}, bf16[256,2048]{1,0:T(8,128)(2,1)S(1)}, u32[]{:S(2)}, u32[]{:S(2)}) collective-permute-start(bf16[256,2048]{1,0:T(8,128)(2,1)} %param.6), channel_id=1, source_target_pairs={{0,8},{4,12},{8,0},{12,4},{16,24},{20,28},{24,16},{28,20},{1,9},{5... | collective-permute-start | bytes 3145736 | tf_op jit(solution)/shard_map/ppermute | solution.py:71
  10.9 1.5 collective-permute-start.6
  13.1 21.2 %collective-permute-done.5 = bf16[256,2048]{1,0:T(8,128)(2,1)S(1)} collective-permute-done((bf16[256,2048]{1,0:T(8,128)(2,1)}, bf16[256,2048]{1,0:T(8,128)(2,1)S(1)}, u32[]{:S(2)}, u32[]{:S(2)}) %collective-permute-start.5) | collective-permute-done | bytes 1048608 | tf_op jit(solution)/shard_map/ppermute | solution.py:71
  34.3 8.1 %convolution_convert_fusion.1 = bf16[896,4096]{1,0:T(8,128)(2,1)} fusion(bf16[1,448,4096]{2,1,0:T(8,128)(2,1)} %param.7, s32[448]{0:T(512)} %bitcast.47, pred[448]{0:T(512)(128)(4,1)S(1)} %iota_compare_fusion.1), kind=kOutput, calls=%fused_computation.4 | convolution fusion | flops 3292807168 | bytes 11012288 | tf_op jit(solution)/shard_map/dot_general | solution.py:18
  42.9 4.4 %broadcast_in_dim.2 = bf16[2048,2048]{1,0:T(8,128)(2,1)} broadcast(bf16[]{:T(256)} %constant.56.clone.1), dimensions={} | broadcast | bytes 8388610 | tf_op jit(solution)/shard_map/broadcast_in_dim | solution.py:85
  48.4 21.0 %reshape.40 = bf16[28,32,64,64]{3,2,1,0:T(8,128)(2,1)} reshape(bf16[896,4096]{1,0:T(8,128)(2,1)} %convolution_convert_fusion.1) | data formatting | bytes 14680064 | tf_op jit(solution)/shard_map/reshape | solution.py:20
  69.3 16.7 %copy.13 = bf16[28,32,64,64]{3,1,2,0:T(8,128)(2,1)} copy(bf16[28,32,64,64]{3,2,1,0:T(8,128)(2,1)} %reshape.40) | data formatting | bytes 14680064 | tf_op jit(solution)/shard_map/reshape | solution.py:20
  86.0 20.8 %reshape.41 = bf16[1792,2048]{1,0:T(8,128)(2,1)} reshape(bf16[28,64,32,64]{3,2,1,0:T(8,128)(2,1)} %bitcast.49) | data formatting | bytes 14680064 | tf_op jit(solution)/shard_map/reshape | solution.py:22
  106.9 1.8 collective-permute-start.10
  108.8 1.5 collective-permute-start.11
  112.4 2.3 constant_dynamic-update-slice_fusion.6
  114.7 6.1 %collective-permute-done.10 = bf16[128,2048]{1,0:T(8,128)(2,1)S(1)} collective-permute-done((bf16[128,2048]{1,0:T(8,128)(2,1)S(1)}, bf16[128,2048]{1,0:T(8,128)(2,1)S(1)}, u32[]{:S(2)}, u32[]{:S(2)}) %collective-permute-start.10) | collective-permute-done | bytes 524320 | tf_op jit(solution)/shard_map/ppermute | solution.py:71
  120.8 1.6 collective-permute-done.11
  122.4 2.3 constant_dynamic-update-slice_fusion.5
  124.7 2.3 constant_dynamic-update-slice_fusion.4
  130.4 19.3 %convolution_convert_fusion = bf16[2048,1792]{1,0:T(8,128)(2,1)} fusion(bf16[2048,2048]{1,0:T(8,128)(2,1)} %constant_dynamic-update-slice_fusion, bf16[1792,2048]{1,0:T(8,128)(2,1)S(1)} %bitcast.52), kind=kOutput, calls=%fused_computation.3 | convolution fusion | flops 15036055552 | bytes 23068672 | tf_op jit(solution)/shard_map/dot_general | solution.py:142
  149.8 5.6 %constant_dynamic-slice_fusion.1 = (bf16[4,1,256,1792]{3,2,1,0:T(8,128)(2,1)}, bf16[4,1,256,1792]{3,2,1,0:T(8,128)(2,1)S(1)}) fusion(bf16[4,2,256,1792]{3,2,1,0:T(8,128)(2,1)} %bitcast.50, s32[]{:T(128)S(6)} %select_n.56, s32[]{:T(128)S(6)} %select_n.57), kind=kLoop, calls=%fused_computation.35 | loop fusion | bytes 14680072 | tf_op jit(solution)/shard_map/jit(dynamic_index_in_dim)/dynamic_slice | solution.py:92
  156.1 9.3 %convolution_convert_fusion.2 = bf16[1024,2048]{1,0:T(8,128)(2,1)} fusion(bf16[1024,1792]{1,0:T(8,128)(2,1)S(1)} %bitcast.57, bf16[1792,2048]{1,0:T(8,128)(2,1)S(1)} %bitcast.54), kind=kOutput, calls=%fused_computation.5 | convolution fusion | flops 7518289920 | bytes 15204352 | tf_op jit(solution)/shard_map/dot_general | solution.py:105
  165.9 7.1 %collective-permute-done = bf16[1024,2048]{1,0:T(8,128)(2,1)} collective-permute-done((bf16[1024,2048]{1,0:T(8,128)(2,1)}, bf16[1024,2048]{1,0:T(8,128)(2,1)}, u32[]{:S(2)}, u32[]{:S(2)}) %collective-permute-start) | collective-permute-done | bytes 4194336 | tf_op jit(solution)/shard_map/ppermute | solution.py:71
  173.0 11.7 %add_convert_fusion = bf16[1024,2048]{1,0:T(8,128)(2,1)S(1)} fusion(bf16[1024,2048]{1,0:T(8,128)(2,1)} %collective-permute-done, bf16[1024,1792]{1,0:T(8,128)(2,1)} %bitcast.56, bf16[1792,2048]{1,0:T(8,128)(2,1)} %reshape.41), kind=kOutput, calls=%fused_computation.2 | convolution fusion | flops 7526678528 | bytes 19398656 | tf_op jit(solution)/shard_map/dot_general | solution.py:105
  185.2 1.3 copy-done.2
  186.6 1.6 collective-permute-start.1
  189.8 22.4 %collective-permute-done.1 = bf16[2,256,1024]{2,1,0:T(8,128)(2,1)} collective-permute-done((bf16[2,256,1024]{2,1,0:T(8,128)(2,1)S(1)}, bf16[2,256,1024]{2,1,0:T(8,128)(2,1)}, u32[]{:S(2)}, u32[]{:S(2)}) %collective-permute-start.1) | collective-permute-done | bytes 1048608 | tf_op jit(solution)/shard_map/ppermute | solution.py:71
  212.2 1.9 fusion.2
  215.3 1.7 fusion.1
  218.8 1.7 collective-permute-start.4
  220.5 21.7 %multiply_bitcast_fusion.refs_2_ = f32[1792,2048]{1,0:T(8,128)} fusion(bf16[2048,2048]{1,0:T(8,128)(2,1)} %constant_dynamic-update-slice_fusion, bf16[2048,1792]{1,0:T(8,128)(2,1)} %all-gather.2.cloned.1.call-done), kind=kOutput, calls=%fused_computation.1 | convolution fusion | flops 15036055552 | bytes 30408704 | tf_op jit(solution)/shard_map/dot_general | solution.py:159
  242.2 19.8 %shard_map.76 = bf16[448,32,128]{2,1,0:T(8,128)(2,1)S(1)} custom-call(s32[448]{0:T(512)S(1)} %bitcast.48, s32[1]{0:T(128)} %bitcast.46.refs_1_, f32[1792,2048]{1,0:T(8,128)} %multiply_bitcast_fusion.refs_2_), custom_call_target="tpu_custom_call" | custom-call | bytes 44040192 | tf_op jit(solution)/shard_map/pallas_call | solution.py:52
  262.0 1.8 copy-done
  263.8 6.8 %broadcast_in_dim_reshape.3 = bf16[1,448,4096]{2,1,0:T(8,128)(2,1)} reshape(bf16[448,32,128]{2,1,0:T(8,128)(2,1)} %copy-done) | data formatting | bytes 7340032 | tf_op jit(solution)/shard_map/broadcast_in_dim;reshape | solution.py:163
  270.6 1.2 fusion.6
  273.1 5.0 %reduce-scatter.2.cloned.1.call-done = bf16[512,1792]{1,0:T(8,128)(2,1)} async-done(((bf16[2048,1792]{1,0:T(8,128)(2,1)}), bf16[512,1792]{1,0:T(8,128)(2,1)}) %reduce-scatter.2.cloned.1.call-update) | async-done | bytes 1835024 | tf_op jit(solution)/shard_map/reduce_scatter | solution.py:141
  (59 shorter events, 15.5 us)
Async XLA Ops:
  7.2 142.6 %all-gather.2.cloned.1.call-start = ((), (), s32[]{:S(2)}) async-start(), calls=%async_computation.1 | async-start | bytes 9175040 | tf_op jit(solution)/shard_map/all_gather | solution.py:133
  7.9 270.2 %reduce-scatter.2.cloned.1.call-start = ((), (), s32[]{:S(2)}) async-start(), calls=%async_computation.2 | async-start | bytes 9175040 | tf_op jit(solution)/shard_map/reduce_scatter | solution.py:141
  7.9 26.4 %collective-permute-start.5 = (bf16[256,2048]{1,0:T(8,128)(2,1)}, bf16[256,2048]{1,0:T(8,128)(2,1)S(1)}, u32[]{:S(2)}, u32[]{:S(2)}) collective-permute-start(bf16[256,2048]{1,0:T(8,128)(2,1)} %param.6), channel_id=1, source_target_pairs={{0,8},{4,12},{8,0},{12,4},{16,24},{20,28},{24,16},{28,20},{1,9},{5... | collective-permute-start | bytes 3145736 | tf_op jit(solution)/shard_map/ppermute | solution.py:71
  10.9 31.4 %collective-permute-start.6 = (bf16[256,2048]{1,0:T(8,128)(2,1)}, bf16[256,2048]{1,0:T(8,128)(2,1)S(1)}, u32[]{:S(2)}, u32[]{:S(2)}) collective-permute-start(bf16[256,2048]{1,0:T(8,128)(2,1)} %param.6), channel_id=1, source_target_pairs={{0,16},{4,20},{8,24},{12,28},{16,0},{20,4},{24,8},{28,12},{1,17},{... | collective-permute-start | bytes 3145736 | tf_op jit(solution)/shard_map/ppermute | solution.py:71
  12.5 99.9 %collective-permute-start.7 = (bf16[256,2048]{1,0:T(8,128)(2,1)}, bf16[256,2048]{1,0:T(8,128)(2,1)}, u32[]{:S(2)}, u32[]{:S(2)}) collective-permute-start(bf16[256,2048]{1,0:T(8,128)(2,1)} %param.6), channel_id=1, source_target_pairs={{0,4},{4,0},{8,12},{12,8},{16,20},{20,16},{24,28},{28,24},{1,5},{5... | collective-permute-start | bytes 3145736 | tf_op jit(solution)/shard_map/ppermute | solution.py:71
  34.3 88.1 %collective-permute-start.8 = (bf16[256,2048]{1,0:T(8,128)(2,1)S(1)}, bf16[256,2048]{1,0:T(8,128)(2,1)}, u32[]{:S(2)}, u32[]{:S(2)}) collective-permute-start(bf16[256,2048]{1,0:T(8,128)(2,1)S(1)} %collective-permute-done.5), channel_id=1, source_target_pairs={{0,4},{4,0},{8,12},{12,8},{16,20},{20,16},{24,28},{28,24},{1,5},{5... | collective-permute-start | bytes 3145736 | tf_op jit(solution)/shard_map/ppermute | solution.py:71
  42.4 4.9 %copy-start.5 = (bf16[256,2048]{1,0:T(8,128)(2,1)S(1)}, bf16[256,2048]{1,0:T(8,128)(2,1)}, u32[]{:S(2)}) copy-start(bf16[256,2048]{1,0:T(8,128)(2,1)} %param.6) | copy-start | bytes 3145732
  42.4 82.3 %collective-permute-start.9 = (bf16[256,2048]{1,0:T(8,128)(2,1)S(1)}, bf16[256,2048]{1,0:T(8,128)(2,1)}, u32[]{:S(2)}, u32[]{:S(2)}) collective-permute-start(bf16[256,2048]{1,0:T(8,128)(2,1)S(1)} %collective-permute-done.6), channel_id=1, source_target_pairs={{0,4},{4,0},{8,12},{12,8},{16,20},{20,16},{24,28},{28,24},{1,5},{5... | collective-permute-start | bytes 3145736 | tf_op jit(solution)/shard_map/ppermute | solution.py:71
  106.9 13.9 %collective-permute-start.10 = (bf16[128,2048]{1,0:T(8,128)(2,1)S(1)}, bf16[128,2048]{1,0:T(8,128)(2,1)S(1)}, u32[]{:S(2)}, u32[]{:S(2)}) collective-permute-start(bf16[128,2048]{1,0:T(8,128)(2,1)S(1)} %slice.18), channel_id=1, source_target_pairs={{0,16},{4,20},{8,24},{12,28},{16,0},{20,4},{24,8},{28,12},{1,17},{... | collective-permute-start | bytes 1572872 | tf_op jit(solution)/shard_map/ppermute | solution.py:71
  108.7 21.6 %slice-start = ((s8[7340032]{0:T(1024)(128)(4,1)}), s8[4194304]{0:T(1024)(128)(4,1)S(1)}, s32[]{:S(2)}) async-start(s8[7340032]{0:T(1024)(128)(4,1)} %bitcast.51), calls=%async_computation.3 | async-start | bytes 8388608
  108.8 13.6 %collective-permute-start.11 = (bf16[128,2048]{1,0:T(8,128)(2,1)S(1)}, bf16[128,2048]{1,0:T(8,128)(2,1)S(1)}, u32[]{:S(2)}, u32[]{:S(2)}) collective-permute-start(bf16[128,2048]{1,0:T(8,128)(2,1)S(1)} %slice.19), channel_id=1, source_target_pairs={{0,8},{4,12},{8,0},{12,4},{16,24},{20,28},{24,16},{28,20},{1,9},{5... | collective-permute-start | bytes 1572872 | tf_op jit(solution)/shard_map/ppermute | solution.py:71
  114.7 15.7 %slice-start.1 = ((s8[7340032]{0:T(1024)(128)(4,1)}), s8[3145728]{0:T(1024)(128)(4,1)S(1)}, s32[]{:S(2)}) async-start(s8[7340032]{0:T(1024)(128)(4,1)} %bitcast.51), calls=%async_computation.4 | async-start | bytes 6291456
  120.8 7.9 %collective-permute-start.12 = (bf16[128,2048]{1,0:T(8,128)(2,1)S(1)}, bf16[128,2048]{1,0:T(8,128)(2,1)S(1)}, u32[]{:S(2)}, u32[]{:S(2)}) collective-permute-start(bf16[128,2048]{1,0:T(8,128)(2,1)S(1)} %collective-permute-done.10), channel_id=1, source_target_pairs={{0,4},{4,0},{8,12},{12,8},{16,20},{20,16},{24,28},{28,24},{1,5},{5... | collective-permute-start | bytes 1572872 | tf_op jit(solution)/shard_map/ppermute | solution.py:71
  122.4 7.2 %collective-permute-start.13 = (bf16[128,2048]{1,0:T(8,128)(2,1)S(1)}, bf16[128,2048]{1,0:T(8,128)(2,1)S(1)}, u32[]{:S(2)}, u32[]{:S(2)}) collective-permute-start(bf16[128,2048]{1,0:T(8,128)(2,1)S(1)} %collective-permute-done.11), channel_id=1, source_target_pairs={{0,4},{4,0},{8,12},{12,8},{16,20},{20,16},{24,28},{28,24},{1,5},{5... | collective-permute-start | bytes 1572872 | tf_op jit(solution)/shard_map/ppermute | solution.py:71
  149.7 5.7 %slice-start.2 = ((s8[7340032]{0:T(1024)(128)(4,1)}), s8[3145728]{0:T(1024)(128)(4,1)S(1)}, s32[]{:S(2)}) async-start(s8[7340032]{0:T(1024)(128)(4,1)} %bitcast.53), calls=%async_computation.5 | async-start | bytes 6291456
  149.7 6.3 %slice-start.3 = ((s8[7340032]{0:T(1024)(128)(4,1)}), s8[4194304]{0:T(1024)(128)(4,1)S(1)}, s32[]{:S(2)}) async-start(s8[7340032]{0:T(1024)(128)(4,1)} %bitcast.53), calls=%async_computation.6 | async-start | bytes 8388608
  165.4 7.6 %collective-permute-start = (bf16[1024,2048]{1,0:T(8,128)(2,1)}, bf16[1024,2048]{1,0:T(8,128)(2,1)}, u32[]{:S(2)}, u32[]{:S(2)}) collective-permute-start(bf16[1024,2048]{1,0:T(8,128)(2,1)} %convolution_convert_fusion.2), channel_id=1, source_target_pairs={{0,4},{4,0},{8,12},{12,8},{16,20},{20,16},{24,28},{28,24},{1,5},{5... | collective-permute-start | bytes 12582920 | tf_op jit(solution)/shard_map/ppermute | solution.py:71
  185.2 1.3 copy-start.2
  186.6 25.6 %collective-permute-start.1 = (bf16[2,256,1024]{2,1,0:T(8,128)(2,1)S(1)}, bf16[2,256,1024]{2,1,0:T(8,128)(2,1)}, u32[]{:S(2)}, u32[]{:S(2)}) collective-permute-start(bf16[2,256,1024]{2,1,0:T(8,128)(2,1)S(1)} %dynamic-slice_bitcast_fusion.1), channel_id=1, source_target_pairs={{0,8},{4,12},{8,0},{12,4},{16,24},{20,28},{24,16},{28,20},{1,9},{5... | collective-permute-start | bytes 3145736 | tf_op jit(solution)/shard_map/ppermute | solution.py:71
  189.2 26.1 %collective-permute-start.3 = (bf16[2,256,1024]{2,1,0:T(8,128)(2,1)}, bf16[2,256,1024]{2,1,0:T(8,128)(2,1)}, u32[]{:S(2)}, u32[]{:S(2)}) collective-permute-start(bf16[2,256,1024]{2,1,0:T(8,128)(2,1)} %dynamic-slice_bitcast_fusion), channel_id=1, source_target_pairs={{0,16},{4,20},{8,24},{12,28},{16,0},{20,4},{24,8},{28,12},{1,17},{... | collective-permute-start | bytes 3145736 | tf_op jit(solution)/shard_map/ppermute | solution.py:71
  215.0 55.5 %collective-permute-start.2 = (bf16[256,1024]{1,0:T(8,128)(2,1)}, bf16[256,1024]{1,0:T(8,128)(2,1)}, u32[]{:S(2)}, u32[]{:S(2)}) collective-permute-start(bf16[256,1024]{1,0:T(8,128)(2,1)} %dynamic-slice_bitcast_fusion.3), channel_id=1, source_target_pairs={{0,16},{4,20},{8,24},{12,28},{16,0},{20,4},{24,8},{28,12},{1,17},{... | collective-permute-start | bytes 1572872 | tf_op jit(solution)/shard_map/ppermute | solution.py:71
  217.0 1.0 copy-start.3
  218.8 23.4 %copy-start.1 = (s32[1,448]{1,0:T(1,128)S(1)}, s32[1,448]{1,0:T(1,128)}, u32[]{:S(2)}) copy-start(s32[1,448]{1,0:T(1,128)} %param.8) | copy-start | bytes 5380
  218.8 53.0 %collective-permute-start.4 = (bf16[256,1024]{1,0:T(8,128)(2,1)}, bf16[256,1024]{1,0:T(8,128)(2,1)S(1)}, u32[]{:S(2)}, u32[]{:S(2)}) collective-permute-start(bf16[256,1024]{1,0:T(8,128)(2,1)} %dynamic-slice_bitcast_fusion.2), channel_id=1, source_target_pairs={{0,8},{4,12},{8,0},{12,4},{16,24},{20,28},{24,16},{28,20},{1,9},{5... | collective-permute-start | bytes 1572872 | tf_op jit(solution)/shard_map/ppermute | solution.py:71
  262.0 1.8 copy-start
  263.8 8.0 %copy-start.4 = (bf16[2,256,1024]{2,1,0:T(8,128)(2,1)S(1)}, bf16[2,256,1024]{2,1,0:T(8,128)(2,1)}, u32[]{:S(2)}) copy-start(bf16[2,256,1024]{2,1,0:T(8,128)(2,1)} %copy-done.3) | copy-start | bytes 3145732
Sparse Core Ops, SparseCore 0:
  9.6 135.1 all-gather.1
  149.8 128.2 reduce-scatter.1

commit v2 on v1

--- a/solution.py
+++ b/solution.py
@@ -8,19 +8,8 @@
 from jax.sharding import PartitionSpec as P
 
 BLOCK = 64
-UNROLL = 4
+UNROLL = 7
 CORE, X, Y = 1, 2, 4
-
-
-def dense_tile(slots, index, live, row_blocks, col_blocks):
-    positions = jnp.arange(row_blocks * col_blocks, dtype=jnp.int32)
-    onehot = ((positions[:, None] == index[None, :]) & live[None, :]).astype(jnp.bfloat16)
-    flat = jnp.dot(onehot, slots, preferred_element_type=jnp.float32).astype(jnp.bfloat16)
-    return (
-        flat.reshape(row_blocks, col_blocks, BLOCK, BLOCK)
-        .transpose(0, 2, 1, 3)
-        .reshape(row_blocks * BLOCK, col_blocks * BLOCK)
-    )
 
 
 def pick_kernel(col_blocks, capacity, index_ref, count_ref, wide_ref, out_ref, pair_ref):
@@ -47,6 +36,58 @@
     lax.fori_loop(0, capacity // UNROLL, step, 0)
 
 
+def build_kernel(col_blocks, capacity, index_ref, count_ref, slot_ref, tile_ref, pair_ref):
+    half = BLOCK // 2
+    lane = lax.broadcasted_iota(jnp.int32, (half, 2 * BLOCK), 1)
+    side = lax.broadcasted_iota(jnp.int32, (BLOCK, 2 * BLOCK), 1) // BLOCK
+    count = count_ref[0]
+
+    def clear(i, carry):
+        top = pl.multiple_of(i * BLOCK, BLOCK)
+        tile_ref[pl.ds(top, BLOCK), :] = jnp.zeros((BLOCK, tile_ref.shape[1]), tile_ref.dtype)
+        return carry
+
+    lax.fori_loop(0, tile_ref.shape[0] // BLOCK, clear, 0)
+
+    def step(i, carry):
+        for u in range(UNROLL):
+            s = i * UNROLL + u
+            k = index_ref[s]
+            top = pl.multiple_of((k // col_blocks) * BLOCK, BLOCK)
+            col = k % col_blocks
+            left = pl.multiple_of((col // 2) * (2 * BLOCK), 2 * BLOCK)
+            v = slot_ref[s].astype(jnp.float32)
+            turned = pltpu.roll(v, BLOCK, 1)
+            pair_ref[u, pl.ds(0, half, stride=2), :] = jnp.where(lane < BLOCK, v, turned)
+            pair_ref[u, pl.ds(1, half, stride=2), :] = jnp.where(lane < BLOCK, turned, v)
+            place = (pl.ds(top, BLOCK), pl.ds(left, 2 * BLOCK))
+            want = jnp.where(s < count, col % 2, 2)
+            old = tile_ref[place].astype(jnp.float32)
+            tile_ref[place] = jnp.where(side == want, pair_ref[u], old).astype(jnp.bfloat16)
+        return carry
+
+    lax.fori_loop(0, capacity // UNROLL, step, 0)
+
+
+def build_tile(slots, index, count, row_blocks, col_blocks):
+    capacity = index.shape[0]
+    return pl.pallas_call(
+        lambda *refs: build_kernel(col_blocks, capacity, *refs),
+        out_shape=jax.ShapeDtypeStruct((row_blocks * BLOCK, col_blocks * BLOCK), jnp.bfloat16),
+        in_specs=[
+            pl.BlockSpec(memory_space=pltpu.SMEM),
+            pl.BlockSpec(memory_space=pltpu.SMEM),
+            pl.BlockSpec(memory_space=pltpu.VMEM),
+        ],
+        out_specs=pl.BlockSpec(memory_space=pltpu.VMEM),
+        scratch_shapes=[pltpu.VMEM((UNROLL, BLOCK, 2 * BLOCK), jnp.float32)],
+        compiler_params=pltpu.CompilerParams(vmem_limit_bytes=40 * 1024 * 1024),
+        cost_estimate=pl.CostEstimate(
+            flops=0, bytes_accessed=16 * slots.size, transcendentals=0
+        ),
+    )(index, count, slots.reshape(capacity, BLOCK // 2, 2 * BLOCK))
+
+
 def pick_blocks(wide, index, count, col_blocks):
     capacity = index.shape[0]
     out = pl.pallas_call(
@@ -71,21 +112,52 @@
     return lax.ppermute(x, "row", [(r, r ^ mask) for r in range(8)])
 
 
-def gather_row(g):
-    me = lax.axis_index("row")
+def gather_both(hidden, g, tile):
+    me, z = lax.axis_index("row"), lax.axis_index("col")
     half = g.shape[0] // 2
     gx, gy = swap(g, X), swap(g, Y)
+    up1 = shift(hidden, 1, 1)
+    down1 = shift(hidden, -1, 1)
+    other = swap(g, CORE)
+    gx, gy, tile = lax.optimization_barrier((gx, gy, tile))
     first = swap(gx[:half], Y)
     last = swap(gy[half:], X)
-    mine = {0: g, X: gx, Y: gy}
-    parts = [(m, 0, p) for m, p in mine.items()]
-    parts += [(m ^ CORE, 0, swap(p, CORE)) for m, p in mine.items()]
+    parts = [(0, 0, g), (X, 0, gx), (Y, 0, gy), (CORE, 0, other)]
+    parts += [(X ^ CORE, 0, swap(gx, CORE)), (Y ^ CORE, 0, swap(gy, CORE))]
+    first, last, up1, down1 = lax.optimization_barrier((first, last, up1, down1))
+    up2 = shift(up1, 1, 2)
+    down2 = shift(down1, -1, 2)
     parts += [(X ^ Y, 0, first), (X ^ Y, half, last)]
     parts += [(X ^ Y ^ CORE, 0, swap(first, CORE)), (X ^ Y ^ CORE, half, swap(last, CORE))]
-    whole = jnp.zeros((8 * g.shape[0], g.shape[1]), g.dtype)
+    g_all = jnp.zeros((8 * g.shape[0], g.shape[1]), g.dtype)
     for m, start, p in parts:
-        whole = lax.dynamic_update_slice(whole, p, ((me ^ m) * g.shape[0] + start, 0))
-    return whole
+        g_all = lax.dynamic_update_slice(g_all, p, ((me ^ m) * g.shape[0] + start, 0))
+    in_part = input_product(g_all, tile)
+    in_part, up2, down2 = lax.optimization_barrier((in_part, up2, down2))
+    up3 = shift(up2, 1, 3)
+    down3 = shift(down2, -1, 3)
+    rows = hidden.shape[0]
+    h_all = jnp.zeros((4 * rows, hidden.shape[1]), hidden.dtype)
+    shards = [hidden]
+    for k, (up, down) in enumerate(((up1, down3), (up2, down2), (up3, down1)), 1):
+        shards.append(jnp.where(z >= k, up, down))
+    for k, p in enumerate(shards):
+        h_all = lax.dynamic_update_slice(h_all, p, (((z - k) & 3) * rows, 0))
+    return h_all, g_all, tile, in_part
+
+
+def shift(x, way, step):
+    if way > 0:
+        pairs = [(i, i + 1) for i in range(step - 1, 3)]
+    else:
+        pairs = [(i, i - 1) for i in range(4 - step, 0, -1)]
+    return lax.ppermute(x, "col", pairs)
+
+
+def input_product(g_all, tile):
+    return lax.dot_general(
+        g_all, tile, (((1,), (1,)), ((), ())), preferred_element_type=jnp.float32
+    ).astype(jnp.bfloat16)
 
 
 def pick(x, i, axis):
@@ -127,25 +199,16 @@
     col_blocks = grad_out.shape[1] // BLOCK
     slots = weight_blocks[0]
     index = block_index[0]
-    filled = block_count[0, 0]
-    capacity = slots.shape[0]
-    live = jnp.arange(capacity, dtype=jnp.int32) < filled
-    h_all = lax.all_gather(hidden, "col", axis=0, tiled=True)
+    tile = build_tile(slots, index, block_count[0], row_blocks, col_blocks)
     if small:
-        g_all = gather_row(grad_out)
+        h_all, g_all, tile, in_part = gather_both(hidden, grad_out, tile)
     else:
+        h_all = lax.all_gather(hidden, "col", axis=0, tiled=True)
         g_all = lax.all_gather(grad_out, "row", axis=0, tiled=True)
+        in_part = input_product(g_all, tile)
     tokens = h_all.shape[0]
     factor = 1.0 / math.sqrt(tokens)
-    tile = dense_tile(slots, index, live, row_blocks, col_blocks)
-    input_grad = lax.psum_scatter(
-        lax.dot_general(
-            g_all, tile, (((1,), (1,)), ((), ())), preferred_element_type=jnp.float32
-        ).astype(jnp.bfloat16),
-        "col",
-        scatter_dimension=0,
-        tiled=True,
-    )
+    input_grad = lax.psum_scatter(in_part, "col", scatter_dimension=0, tiled=True)
     if small:
         output = project_scatter_row(h_all, tile)
     else:
@@ -164,7 +227,7 @@
 
 
 def solution(mesh):
-    small = mesh.shape["row"] == 8
+    small = mesh.shape["row"] == 8 and mesh.shape["col"] == 4
 
     def local(*args):
         return body(small, *args)

time: 287 us -> 360 us (1.25)
  waiting for transfers between devices: 64.1 us -> 165 us
  local copies, waits for them, and re-layouts: 96.8 us -> 50.4 us
  other arithmetic: 6.1 us -> 19.5 us
  matrix products: 70.1 us -> 61.6 us
  starting transfers between devices: 13.1 us -> 20.9 us
  Pallas kernels: 19.8 us -> 26.3 us
    ppermute x0 -> x6, waiting for transfers between devices: none -> 126 us  [shift(): return lax.ppermute(x, 'col', pairs)]
    reshape x3 -> x0, local copies, waits for them, and re-layouts: 58.4 us -> none  [the longest x2 37.6 us: dense_tile(): flat.reshape(row_blocks, col_blocks, BLOCK, BLOCK).transpose(0, 2, 1, 3)]
    ppermute x14, waiting for transfers between devices: 58.4 us -> 39.9 us  [swap(): return lax.ppermute(x, 'row', [(r, r ^ mask) for r in range(8)])]
    ppermute x0 -> x6, starting transfers between devices: none -> 13.5 us  [shift(): return lax.ppermute(x, 'col', pairs)]
    pallas_call x0 -> x1, Pallas kernels: none -> 10.2 us  [build_tile(): pl.pallas_call(lambda *refs: build_kernel(col_blocks, capacity, *refs), o...]
    dynamic_update_slice x0 -> x3, other arithmetic: none -> 9.65 us  [gather_both(): h_all = lax.dynamic_update_slice(h_all, p, ((z - k & 3) * rows, 0))]
    dot_general x2 -> x1, matrix products: 27.4 us -> 19.4 us  [input_product(): lax.dot_general(g_all, tile, (((1,), (1,)), ((), ())), preferred_element_...]
    ppermute x14, starting transfers between devices: 13.1 us -> 7.28 us  [swap(): return lax.ppermute(x, 'row', [(r, r ^ mask) for r in range(8)])]
  transfers between devices with their start and end apart: 16 -> 21, of which waited for: 6 -> 5; matrix products, arithmetic and copies ran while one was open for 59% -> 35% of each run, Pallas kernels for 7% -> 7%
where the time goes in v2:
time: 360 us; the launch traced here: 359 us
  waiting for transfers between devices  165 us (46%)
  matrix products  61.6 us (17%)
  local copies, waits for them, and re-layouts  50.4 us (14%)
  Pallas kernels  26.3 us (7%)
  starting transfers between devices  20.9 us (6%)
  other arithmetic  19.5 us (5%)
  between operations  14.9 us (4%)
    ppermute x6, waiting for transfers between devices, shift(): return lax.ppermute(x, 'col', pairs)  126 us
    ppermute x14, waiting for transfers between devices, swap(): return lax.ppermute(x, 'row', [(r, r ^ mask) for r in range(8)])  39.9 us
    dot_general x1, matrix products, body(): lax.dot_general(h_all, g_all, (((0,), (0,)), ((), ())), preferred_element...  21.6 us
    dot_general x2, matrix products, product(): jnp.dot(rows, tile, preferred_element_type=jnp.float32).astype(jnp.bfloat16)  20.6 us
    dot_general x1, matrix products, input_product(): lax.dot_general(g_all, tile, (((1,), (1,)), ((), ())), preferred_element_...  19.4 us
    pallas_call x1, Pallas kernels, pick_blocks(): pl.pallas_call(lambda *refs: pick_kernel(col_blocks, capacity, *refs), ou...  16.1 us
    dynamic_update_slice x10, local copies, waits for them, and re-layouts, gather_both(): lax.dynamic_update_slice(g_all, p, ((me ^ m) * g.shape[0] + start, 0))  14.5 us
    ppermute x6, starting transfers between devices, shift(): return lax.ppermute(x, 'col', pairs)  13.5 us
  transfers between devices with their start and end apart: 21, of which 5 were waited for; matrix products, arithmetic and copies ran while one was open for 35% of the time, Pallas kernels for 7%

profile of v2, /device:TPU:0, one launch (start us, length us, event | category | flops | bytes accessed | tf_op | source)
XLA Modules:
  0.0 359.0 jit_solution(4813451265346323524)
XLA Ops:
  7.2 3.0 collective-permute-start.1
  13.0 5.8 %collective-permute-start.4 = (bf16[512,1792]{1,0:T(8,128)(2,1)}, bf16[512,1792]{1,0:T(8,128)(2,1)}, u32[]{:S(2)}, u32[]{:S(2)}) collective-permute-start(bf16[512,1792]{1,0:T(8,128)(2,1)} %param.5), channel_id=1, source_target_pairs={{0,1},{1,2},{2,3},{4,5},{5,6},{6,7},{8,9},{9,10},{10,11},{12,13},{... | collective-permute-start | bytes 5505032 | tf_op jit(solution)/shard_map/ppermute | solution.py:154
  19.5 3.1 copy.8
  22.6 10.2 %shard_map.76 = bf16[1792,2048]{1,0:T(8,128)(2,1)S(1)} custom-call(s32[448]{0:T(512)S(1)} %bitcast.44, s32[1]{0:T(128)} %bitcast.37.refs_1_, bf16[448,32,128]{2,1,0:T(8,128)(2,1)S(1)} %bitcast.39), custom_call_target="tpu_custom_call" | custom-call | bytes 29360128 | tf_op jit(solution)/shard_map/pallas_call | solution.py:74
  32.8 2.9 copy-done.1
  37.9 4.3 %broadcast_in_dim.7 = bf16[2048,2048]{1,0:T(8,128)(2,1)} broadcast(bf16[]{:T(256)} %constant.57.clone.1), dimensions={} | broadcast | bytes 8388610 | tf_op jit(solution)/shard_map/broadcast_in_dim | solution.py:132
  43.3 7.3 %collective-permute-done.3 = bf16[128,2048]{1,0:T(8,128)(2,1)} collective-permute-done((bf16[128,2048]{1,0:T(8,128)(2,1)}, bf16[128,2048]{1,0:T(8,128)(2,1)}, u32[]{:S(2)}, u32[]{:S(2)}) %collective-permute-start.3) | collective-permute-done | bytes 524320 | tf_op jit(solution)/shard_map/ppermute | solution.py:112
  53.2 2.3 constant_dynamic-update-slice_fusion.6
  55.5 8.0 %collective-permute-done.2 = bf16[128,2048]{1,0:T(8,128)(2,1)S(1)} collective-permute-done((bf16[128,2048]{1,0:T(8,128)(2,1)S(1)}, bf16[128,2048]{1,0:T(8,128)(2,1)S(1)}, u32[]{:S(2)}, u32[]{:S(2)}) %collective-permute-start.2) | collective-permute-done | bytes 524320 | tf_op jit(solution)/shard_map/ppermute | solution.py:112
  64.1 2.0 collective-permute-start.11
  67.3 2.3 constant_dynamic-update-slice_fusion.5
  69.7 2.3 constant_dynamic-update-slice_fusion.4
  72.8 1.9 constant_dynamic-update-slice_fusion.2
  76.4 19.4 %convolution_convert_fusion = bf16[2048,1792]{1,0:T(8,128)(2,1)} fusion(bf16[2048,2048]{1,0:T(8,128)(2,1)} %constant_dynamic-update-slice_fusion, bf16[1792,2048]{1,0:T(8,128)(2,1)S(1)} %bitcast.41), kind=kOutput, calls=%fused_computation.2 | convolution fusion | flops 15036055552 | bytes 23068672 | tf_op jit(solution)/shard_map/dot_general | solution.py:158
  95.8 16.9 %collective-permute-done.12 = bf16[512,1792]{1,0:T(8,128)(2,1)} collective-permute-done((bf16[512,1792]{1,0:T(8,128)(2,1)}, bf16[512,1792]{1,0:T(8,128)(2,1)}, u32[]{:S(2)}, u32[]{:S(2)}) %collective-permute-start.12) | collective-permute-done | bytes 1835040 | tf_op jit(solution)/shard_map/ppermute | solution.py:154
  114.0 1.9 collective-permute-start.14
  115.9 3.5 broadcast_in_dim.6
  120.8 108.6 %collective-permute-done.13 = bf16[512,1792]{1,0:T(8,128)(2,1)} collective-permute-done((bf16[512,1792]{1,0:T(8,128)(2,1)}, bf16[512,1792]{1,0:T(8,128)(2,1)}, u32[]{:S(2)}, u32[]{:S(2)}) %collective-permute-start.13) | collective-permute-done | bytes 1835040 | tf_op jit(solution)/shard_map/ppermute | solution.py:154
  229.4 3.2 select_dynamic-update-slice_fusion.2
  232.6 3.2 select_dynamic-update-slice_fusion.1
  235.8 3.3 select_dynamic-update-slice_fusion
  239.1 5.8 %constant_dynamic-slice_fusion.1 = (bf16[4,1,256,1792]{3,2,1,0:T(8,128)(2,1)}, bf16[4,1,256,1792]{3,2,1,0:T(8,128)(2,1)S(1)}) fusion(bf16[4,2,256,1792]{3,2,1,0:T(8,128)(2,1)} %bitcast.2, s32[]{:T(128)S(6)} %select_n.108, s32[]{:T(128)S(6)} %select_n.109), kind=kLoop, calls=%fused_computation.21 | loop fusion | bytes 14680072 | tf_op jit(solution)/shard_map/jit(dynamic_index_in_dim)/dynamic_slice | solution.py:164
  244.8 9.5 %convolution_convert_fusion.1 = bf16[1024,2048]{1,0:T(8,128)(2,1)} fusion(bf16[1024,1792]{1,0:T(8,128)(2,1)S(1)} %bitcast.49, bf16[1792,2048]{1,0:T(8,128)(2,1)S(1)} %bitcast.43), kind=kOutput, calls=%fused_computation.3 | convolution fusion | flops 7518289920 | bytes 15204352 | tf_op jit(solution)/shard_map/dot_general | solution.py:177
  254.3 11.1 %fusion.5 = bf16[1024,2048]{1,0:T(8,128)(2,1)S(1)} fusion(bf16[1024,1792]{1,0:T(8,128)(2,1)} %bitcast.48, bf16[1792,2048]{1,0:T(8,128)(2,1)} %copy-done.1), kind=kOutput, calls=%fused_computation.34 | convolution fusion | flops 7516192768 | bytes 15204352 | tf_op jit(solution)/shard_map/dot_general | solution.py:177
  265.4 3.7 %add_convert_fusion = bf16[1024,2048]{1,0:T(8,128)(2,1)S(1)} fusion(bf16[1024,2048]{1,0:T(8,128)(2,1)} %collective-permute-done.15, bf16[1024,2048]{1,0:T(8,128)(2,1)S(1)} %fusion.5), kind=kLoop, calls=%fused_computation.1 | loop fusion | flops 8388608 | bytes 12582912 | tf_op jit(solution)/shard_map/convert_element_type | solution.py:181
  272.1 24.6 %collective-permute-done.18 = bf16[2,256,1024]{2,1,0:T(8,128)(2,1)} collective-permute-done((bf16[2,256,1024]{2,1,0:T(8,128)(2,1)S(1)}, bf16[2,256,1024]{2,1,0:T(8,128)(2,1)}, u32[]{:S(2)}, u32[]{:S(2)}) %collective-permute-start.18) | collective-permute-done | bytes 1048608 | tf_op jit(solution)/shard_map/ppermute | solution.py:112
  296.7 1.9 fusion
  299.5 1.6 fusion.1
  303.3 21.6 %convolution_multiply_fusion.refs_2_ = f32[1792,2048]{1,0:T(8,128)} fusion(bf16[2048,1792]{1,0:T(8,128)(2,1)} %select_dynamic-update-slice_fusion, bf16[2048,2048]{1,0:T(8,128)(2,1)} %constant_dynamic-update-slice_fusion), kind=kOutput, calls=%fused_computation | convolution fusion | flops 15036055552 | bytes 30408704 | tf_op jit(solution)/shard_map/dot_general | solution.py:222
  324.9 16.1 %shard_map.77 = bf16[448,32,128]{2,1,0:T(8,128)(2,1)S(1)} custom-call(s32[448]{0:T(512)S(1)} %bitcast.45, s32[1]{0:T(128)} %bitcast.38.refs_1_, f32[1792,2048]{1,0:T(8,128)} %convolution_multiply_fusion.refs_2_), custom_call_target="tpu_custom_call" | custom-call | bytes 44040192 | tf_op jit(solution)/shard_map/pallas_call | solution.py:93
  341.0 1.8 copy-done
  342.8 6.8 %broadcast_in_dim_reshape.3 = bf16[1,448,4096]{2,1,0:T(8,128)(2,1)} reshape(bf16[448,32,128]{2,1,0:T(8,128)(2,1)} %copy-done) | data formatting | bytes 7340032 | tf_op jit(solution)/shard_map/broadcast_in_dim;reshape | solution.py:226
  (75 shorter events, 24.1 us)
Async XLA Ops:
  7.2 15.4 %copy-start.2 = (s32[1,448]{1,0:T(1,128)S(1)}, s32[1,448]{1,0:T(1,128)}, u32[]{:S(2)}) copy-start(s32[1,448]{1,0:T(1,128)} %param.8) | copy-start | bytes 5380
  7.2 344.9 %reduce-scatter.2.cloned.1.call-start = ((), (), s32[]{:S(2)}) async-start(), calls=%async_computation.1 | async-start | bytes 9175040 | tf_op jit(solution)/shard_map/reduce_scatter | solution.py:211
  7.2 28.5 %collective-permute-start.1 = (bf16[256,2048]{1,0:T(8,128)(2,1)}, bf16[256,2048]{1,0:T(8,128)(2,1)S(1)}, u32[]{:S(2)}, u32[]{:S(2)}) collective-permute-start(bf16[256,2048]{1,0:T(8,128)(2,1)} %param.6), channel_id=1, source_target_pairs={{0,16},{4,20},{8,24},{12,28},{16,0},{20,4},{24,8},{28,12},{1,17},{... | collective-permute-start | bytes 3145736 | tf_op jit(solution)/shard_map/ppermute | solution.py:112
  10.3 25.4 %collective-permute-start = (bf16[256,2048]{1,0:T(8,128)(2,1)}, bf16[256,2048]{1,0:T(8,128)(2,1)S(1)}, u32[]{:S(2)}, u32[]{:S(2)}) collective-permute-start(bf16[256,2048]{1,0:T(8,128)(2,1)} %param.6), channel_id=1, source_target_pairs={{0,8},{4,12},{8,0},{12,4},{16,24},{20,28},{24,16},{28,20},{1,9},{5... | collective-permute-start | bytes 3145736 | tf_op jit(solution)/shard_map/ppermute | solution.py:112
  11.7 25.7 %collective-permute-start.6 = (bf16[256,2048]{1,0:T(8,128)(2,1)}, bf16[256,2048]{1,0:T(8,128)(2,1)}, u32[]{:S(2)}, u32[]{:S(2)}) collective-permute-start(bf16[256,2048]{1,0:T(8,128)(2,1)} %param.6), channel_id=1, source_target_pairs={{0,4},{4,0},{8,12},{12,8},{16,20},{20,16},{24,28},{28,24},{1,5},{5... | collective-permute-start | bytes 3145736 | tf_op jit(solution)/shard_map/ppermute | solution.py:112
  11.7 51.8 %collective-permute-start.5 = (bf16[512,1792]{1,0:T(8,128)(2,1)}, bf16[512,1792]{1,0:T(8,128)(2,1)}, u32[]{:S(2)}, u32[]{:S(2)}) collective-permute-start(bf16[512,1792]{1,0:T(8,128)(2,1)} %param.5), channel_id=1, source_target_pairs={{3,2},{2,1},{1,0},{7,6},{6,5},{5,4},{11,10},{10,9},{9,8},{15,14},{... | collective-permute-start | bytes 5505032 | tf_op jit(solution)/shard_map/ppermute | solution.py:154
  13.0 50.5 %collective-permute-start.4 = (bf16[512,1792]{1,0:T(8,128)(2,1)}, bf16[512,1792]{1,0:T(8,128)(2,1)}, u32[]{:S(2)}, u32[]{:S(2)}) collective-permute-start(bf16[512,1792]{1,0:T(8,128)(2,1)} %param.5), channel_id=1, source_target_pairs={{0,1},{1,2},{2,3},{4,5},{5,6},{6,7},{8,9},{9,10},{10,11},{12,13},{... | collective-permute-start | bytes 5505032 | tf_op jit(solution)/shard_map/ppermute | solution.py:154
  32.8 2.9 copy-start.1
  35.7 6.5 %copy-start.7 = (bf16[256,2048]{1,0:T(8,128)(2,1)S(1)}, bf16[256,2048]{1,0:T(8,128)(2,1)}, u32[]{:S(2)}) copy-start(bf16[256,2048]{1,0:T(8,128)(2,1)} %param.6) | copy-start | bytes 3145732
  36.5 14.1 %collective-permute-start.3 = (bf16[128,2048]{1,0:T(8,128)(2,1)}, bf16[128,2048]{1,0:T(8,128)(2,1)}, u32[]{:S(2)}, u32[]{:S(2)}) collective-permute-start(bf16[128,2048]{1,0:T(8,128)(2,1)} %slice.13), channel_id=1, source_target_pairs={{0,8},{4,12},{8,0},{12,4},{16,24},{20,28},{24,16},{28,20},{1,9},{5... | collective-permute-start | bytes 1572872 | tf_op jit(solution)/shard_map/ppermute | solution.py:112
  37.4 28.7 %collective-permute-start.7 = (bf16[256,2048]{1,0:T(8,128)(2,1)S(1)}, bf16[256,2048]{1,0:T(8,128)(2,1)}, u32[]{:S(2)}, u32[]{:S(2)}) collective-permute-start(bf16[256,2048]{1,0:T(8,128)(2,1)S(1)} %collective-permute-done), channel_id=1, source_target_pairs={{0,4},{4,0},{8,12},{12,8},{16,20},{20,16},{24,28},{28,24},{1,5},{5... | collective-permute-start | bytes 3145736 | tf_op jit(solution)/shard_map/ppermute | solution.py:112
  37.4 32.3 %collective-permute-start.8 = (bf16[256,2048]{1,0:T(8,128)(2,1)S(1)}, bf16[256,2048]{1,0:T(8,128)(2,1)}, u32[]{:S(2)}, u32[]{:S(2)}) collective-permute-start(bf16[256,2048]{1,0:T(8,128)(2,1)S(1)} %collective-permute-done.1), channel_id=1, source_target_pairs={{0,4},{4,0},{8,12},{12,8},{16,20},{20,16},{24,28},{28,24},{1,5},{5... | collective-permute-start | bytes 3145736 | tf_op jit(solution)/shard_map/ppermute | solution.py:112
  43.3 33.1 %slice-start = ((s8[7340032]{0:T(1024)(128)(4,1)}), s8[4194304]{0:T(1024)(128)(4,1)S(1)}, s32[]{:S(2)}) async-start(s8[7340032]{0:T(1024)(128)(4,1)} %bitcast.40), calls=%async_computation.2 | async-start | bytes 8388608
  50.6 12.9 %collective-permute-start.2 = (bf16[128,2048]{1,0:T(8,128)(2,1)S(1)}, bf16[128,2048]{1,0:T(8,128)(2,1)S(1)}, u32[]{:S(2)}, u32[]{:S(2)}) collective-permute-start(bf16[128,2048]{1,0:T(8,128)(2,1)S(1)} %slice.12), channel_id=1, source_target_pairs={{0,16},{4,20},{8,24},{12,28},{16,0},{20,4},{24,8},{28,12},{1,17},{... | collective-permute-start | bytes 1572872 | tf_op jit(solution)/shard_map/ppermute | solution.py:112
  55.5 20.9 %slice-start.1 = ((s8[7340032]{0:T(1024)(128)(4,1)}), s8[3145728]{0:T(1024)(128)(4,1)S(1)}, s32[]{:S(2)}) async-start(s8[7340032]{0:T(1024)(128)(4,1)} %bitcast.40), calls=%async_computation.3 | async-start | bytes 6291456
  63.6 11.2 %collective-permute-start.9 = (bf16[128,2048]{1,0:T(8,128)(2,1)S(1)}, bf16[128,2048]{1,0:T(8,128)(2,1)S(1)}, u32[]{:S(2)}, u32[]{:S(2)}) collective-permute-start(bf16[128,2048]{1,0:T(8,128)(2,1)S(1)} %collective-permute-done.2), channel_id=1, source_target_pairs={{0,4},{4,0},{8,12},{12,8},{16,20},{20,16},{24,28},{28,24},{1,5},{5... | collective-permute-start | bytes 1572872 | tf_op jit(solution)/shard_map/ppermute | solution.py:112
  63.6 12.0 %collective-permute-start.10 = (bf16[128,2048]{1,0:T(8,128)(2,1)}, bf16[128,2048]{1,0:T(8,128)(2,1)S(1)}, u32[]{:S(2)}, u32[]{:S(2)}) collective-permute-start(bf16[128,2048]{1,0:T(8,128)(2,1)} %collective-permute-done.3), channel_id=1, source_target_pairs={{0,4},{4,0},{8,12},{12,8},{16,20},{20,16},{24,28},{28,24},{1,5},{5... | collective-permute-start | bytes 1572872 | tf_op jit(solution)/shard_map/ppermute | solution.py:112
  64.1 31.7 %collective-permute-start.11 = (bf16[512,1792]{1,0:T(8,128)(2,1)}, bf16[512,1792]{1,0:T(8,128)(2,1)}, u32[]{:S(2)}, u32[]{:S(2)}) collective-permute-start(bf16[512,1792]{1,0:T(8,128)(2,1)} %collective-permute-done.4), channel_id=1, source_target_pairs={{1,2},{2,3},{5,6},{6,7},{9,10},{10,11},{13,14},{14,15},{17,18},{18... | collective-permute-start | bytes 5505032 | tf_op jit(solution)/shard_map/ppermute | solution.py:154
  66.1 46.6 %collective-permute-start.12 = (bf16[512,1792]{1,0:T(8,128)(2,1)}, bf16[512,1792]{1,0:T(8,128)(2,1)}, u32[]{:S(2)}, u32[]{:S(2)}) collective-permute-start(bf16[512,1792]{1,0:T(8,128)(2,1)} %collective-permute-done.5), channel_id=1, source_target_pairs={{2,1},{1,0},{6,5},{5,4},{10,9},{9,8},{14,13},{13,12},{18,17},{17,1... | collective-permute-start | bytes 5505032 | tf_op jit(solution)/shard_map/ppermute | solution.py:154
  95.8 23.6 %copy-start.6 = (bf16[512,1792]{1,0:T(8,128)(2,1)S(1)}, bf16[512,1792]{1,0:T(8,128)(2,1)}, u32[]{:S(2)}) copy-start(bf16[512,1792]{1,0:T(8,128)(2,1)} %param.5) | copy-start | bytes 5505028
  112.7 116.7 %collective-permute-start.13 = (bf16[512,1792]{1,0:T(8,128)(2,1)}, bf16[512,1792]{1,0:T(8,128)(2,1)}, u32[]{:S(2)}, u32[]{:S(2)}) collective-permute-start(bf16[512,1792]{1,0:T(8,128)(2,1)} %collective-permute-done.12), channel_id=1, source_target_pairs={{1,0},{5,4},{9,8},{13,12},{17,16},{21,20},{25,24},{29,28}} | collective-permute-start | bytes 5505032 | tf_op jit(solution)/shard_map/ppermute | solution.py:154
  114.0 121.8 %collective-permute-start.14 = (bf16[512,1792]{1,0:T(8,128)(2,1)}, bf16[512,1792]{1,0:T(8,128)(2,1)}, u32[]{:S(2)}, u32[]{:S(2)}) collective-permute-start(bf16[512,1792]{1,0:T(8,128)(2,1)} %collective-permute-done.11), channel_id=1, source_target_pairs={{2,3},{6,7},{10,11},{14,15},{18,19},{22,23},{26,27},{30,31}} | collective-permute-start | bytes 5505032 | tf_op jit(solution)/shard_map/ppermute | solution.py:154
  235.8 9.1 %slice-start.2 = ((s8[7340032]{0:T(1024)(128)(4,1)}), s8[4194304]{0:T(1024)(128)(4,1)S(1)}, s32[]{:S(2)}) async-start(s8[7340032]{0:T(1024)(128)(4,1)} %bitcast.42), calls=%async_computation.4 | async-start | bytes 8388608
  239.0 5.8 %slice-start.3 = ((s8[7340032]{0:T(1024)(128)(4,1)}), s8[3145728]{0:T(1024)(128)(4,1)S(1)}, s32[]{:S(2)}) async-start(s8[7340032]{0:T(1024)(128)(4,1)} %bitcast.42), calls=%async_computation.5 | async-start | bytes 6291456
  254.3 11.1 %collective-permute-start.15 = (bf16[1024,2048]{1,0:T(8,128)(2,1)}, bf16[1024,2048]{1,0:T(8,128)(2,1)}, u32[]{:S(2)}, u32[]{:S(2)}) collective-permute-start(bf16[1024,2048]{1,0:T(8,128)(2,1)} %convolution_convert_fusion.1), channel_id=1, source_target_pairs={{0,4},{4,0},{8,12},{12,8},{16,20},{20,16},{24,28},{28,24},{1,5},{5... | collective-permute-start | bytes 12582920 | tf_op jit(solution)/shard_map/ppermute | solution.py:112
  269.6 1.3 copy-start.3
  271.0 25.7 %collective-permute-start.18 = (bf16[2,256,1024]{2,1,0:T(8,128)(2,1)S(1)}, bf16[2,256,1024]{2,1,0:T(8,128)(2,1)}, u32[]{:S(2)}, u32[]{:S(2)}) collective-permute-start(bf16[2,256,1024]{2,1,0:T(8,128)(2,1)S(1)} %dynamic-slice_bitcast_fusion), channel_id=1, source_target_pairs={{0,16},{4,20},{8,24},{12,28},{16,0},{20,4},{24,8},{28,12},{1,17},{... | collective-permute-start | bytes 3145736 | tf_op jit(solution)/shard_map/ppermute | solution.py:112
  272.1 27.4 %collective-permute-start.16 = (bf16[2,256,1024]{2,1,0:T(8,128)(2,1)}, bf16[2,256,1024]{2,1,0:T(8,128)(2,1)}, u32[]{:S(2)}, u32[]{:S(2)}) collective-permute-start(bf16[2,256,1024]{2,1,0:T(8,128)(2,1)} %dynamic-slice_bitcast_fusion.1), channel_id=1, source_target_pairs={{0,8},{4,12},{8,0},{12,4},{16,24},{20,28},{24,16},{28,20},{1,9},{5... | collective-permute-start | bytes 3145736 | tf_op jit(solution)/shard_map/ppermute | solution.py:112
  299.5 50.0 %collective-permute-start.19 = (bf16[256,1024]{1,0:T(8,128)(2,1)}, bf16[256,1024]{1,0:T(8,128)(2,1)}, u32[]{:S(2)}, u32[]{:S(2)}) collective-permute-start(bf16[256,1024]{1,0:T(8,128)(2,1)} %dynamic-slice_bitcast_fusion.2), channel_id=1, source_target_pairs={{0,8},{4,12},{8,0},{12,4},{16,24},{20,28},{24,16},{28,20},{1,9},{5... | collective-permute-start | bytes 1572872 | tf_op jit(solution)/shard_map/ppermute | solution.py:112
  303.0 47.8 %collective-permute-start.17 = (bf16[256,1024]{1,0:T(8,128)(2,1)}, bf16[256,1024]{1,0:T(8,128)(2,1)S(1)}, u32[]{:S(2)}, u32[]{:S(2)}) collective-permute-start(bf16[256,1024]{1,0:T(8,128)(2,1)} %dynamic-slice_bitcast_fusion.3), channel_id=1, source_target_pairs={{0,16},{4,20},{8,24},{12,28},{16,0},{20,4},{24,8},{28,12},{1,17},{... | collective-permute-start | bytes 1572872 | tf_op jit(solution)/shard_map/ppermute | solution.py:112
  341.0 1.8 copy-start
  342.8 8.0 %copy-start.5 = (bf16[2,256,1024]{2,1,0:T(8,128)(2,1)S(1)}, bf16[2,256,1024]{2,1,0:T(8,128)(2,1)}, u32[]{:S(2)}) copy-start(bf16[2,256,1024]{2,1,0:T(8,128)(2,1)} %copy-done.4) | copy-start | bytes 3145732
  (1 other events, 1.0 us)
Sparse Core Ops, SparseCore 0:
  120.9 154.7 reduce-scatter.1
